TPU v7x, 32 devices: a whole 2x2x4 slice. The times are simulated.
32 devices in a mesh: blk: 32 (over z, y, x, core).
Axes of the slice: x: 2, y: 2, z: 4, core: 2. Of those that a mesh axis runs over, the one named last changes fastest.
Arguments:
- points: float32 [49152, 128], P('blk'), may hold values from -6 to 6
- inv_scale: float32 [128], replicated, may hold values from 0.03 to 0.3
- vectors: float32 [49152, 64], P('blk'), may hold values from -6 to 6
Outputs:
- product: float32 [49152, 64], P('blk')
All inputs are finite; a program needn't handle non-finite values.
Results may differ from a plain program's by a relative error of at most 0.0003.
Values sent between devices are 32-bit elements; how exact they have to be, the bound alone decides.
A program may use at most 64 MiB of HBM per device.

v0:
```python
import functools

import jax
import jax.numpy as jnp
from jax import lax
from jax.experimental import pallas as pl
from jax.experimental.pallas import tpu as pltpu
from jax.sharding import PartitionSpec as P

AXIS = "blk"
CHUNK = 256
OWN, MATE, FAR = 0, 1, 2
MESH = pl.DeviceIdType.MESH
F32, BF16 = jnp.float32, jnp.bfloat16


def split(x):
    high = x.astype(BF16)
    return high, (x - high.astype(F32)).astype(BF16)


def dot(a, b):
    return lax.dot_general(a, b, (((1,), (0,)), ((), ())), preferred_element_type=F32)


def dot_nt(a, b):
    return lax.dot_general(a, b, (((1,), (1,)), ((), ())), preferred_element_type=F32)


def fold(wide):
    half = wide.shape[0] // 2
    return wide[:half] + wide[half:]


def kernel(
    n, p_ref, s_ref, v_ref, o_ref,
    send, far_in, mate_in, left, right, vec, vec_t, sq_col, sq_row, acc_t, out_t,
    far_part, mate_part, far_back, mate_back,
    far_send_sem, far_recv_sem, mate_send_sem, mate_recv_sem,
    part_send_sem, part_recv_sem, mpart_send_sem, mpart_recv_sem,
):
    chunks = p_ref.shape[0] // CHUNK
    feat = p_ref.shape[1]
    cols = v_ref.shape[1]
    me = lax.axis_index(AXIS)
    odd = lax.rem(me, 2)
    even = odd == 0
    up, down = lax.rem(me + 2, n), lax.rem(me + n - 2, n)
    mate = me + 1 - 2 * odd
    host = jnp.where(even, down, up)
    guest = jnp.where(even, up, down)

    barrier = pltpu.get_barrier_semaphore()
    for other in (mate, up, down):
        pl.semaphore_signal(barrier, inc=1, device_id=(other,), device_id_type=MESH)

    def place(slot, c, scaled, vt):
        high, low = split(scaled)
        left[slot, c] = jnp.concatenate([high, low, high, low], axis=1)
        right[slot, c] = jnp.concatenate([high, low, low, high], axis=1)
        held = high.astype(F32) + low.astype(F32)
        squares = held * held
        sq_col[slot, c] = jnp.broadcast_to(
            -0.5 * jnp.sum(squares, axis=1, keepdims=True), (CHUNK, 128)
        )
        sq_row[slot, c] = jnp.broadcast_to(
            -0.5 * jnp.sum(squares.T, axis=0, keepdims=True), (8, CHUNK)
        )
        vt_high, vt_low = split(vt)
        vec_t[slot, c] = jnp.concatenate([vt_high, vt_low], axis=0)
        v_high, v_low = split(vt.T)
        vec[slot, c] = jnp.concatenate([v_high, v_low], axis=1)

    def place_packed(slot, c, source):
        scaled = source[c, :CHUNK]
        vt = jnp.concatenate(
            [source[c, CHUNK : CHUNK + cols], source[c, CHUNK + cols :]], axis=1
        )
        place(slot, c, scaled, vt)

    scale = s_ref[...]

    def prepare(c, carry):
        rows = pl.ds(pl.multiple_of(c * CHUNK, CHUNK), CHUNK)
        scaled = p_ref[rows, :] * scale
        vt = v_ref[rows, :].T
        send[c, :CHUNK] = scaled
        send[c, CHUNK : CHUNK + cols] = vt[:, :128]
        send[c, CHUNK + cols :] = vt[:, 128:]
        place(OWN, c, scaled, vt)
        return carry

    lax.fori_loop(0, chunks, prepare, 0)
    acc_t[...] = jnp.zeros_like(acc_t)

    pl.semaphore_wait(barrier, 3)

    def far_copy(c):
        return pltpu.make_async_remote_copy(
            src_ref=send.at[c], dst_ref=far_in.at[c],
            send_sem=far_send_sem.at[c], recv_sem=far_recv_sem.at[c],
            device_id=(host,), device_id_type=MESH,
        )

    def part_copy(c):
        return pltpu.make_async_remote_copy(
            src_ref=far_part.at[c], dst_ref=far_back.at[c],
            send_sem=part_send_sem.at[c], recv_sem=part_recv_sem.at[c],
            device_id=(guest,), device_id_type=MESH,
        )

    mate_copy = pltpu.make_async_remote_copy(
        src_ref=send, dst_ref=mate_in, send_sem=mate_send_sem, recv_sem=mate_recv_sem,
        device_id=(mate,), device_id_type=MESH,
    )
    mpart_copy = pltpu.make_async_remote_copy(
        src_ref=mate_part, dst_ref=mate_back, send_sem=mpart_send_sem,
        recv_sem=mpart_recv_sem, device_id=(mate,), device_id_type=MESH,
    )
    for c in range(chunks):
        far_copy(c).start()
    mate_copy.start()

    def tile(a, c, b, mirrored):
        rows = left[a, c]
        col = jnp.concatenate([sq_col[a, c]] * (CHUNK // 128), axis=1)
        rows_vec = vec_t[a, c]
        total = jnp.zeros((CHUNK, 2 * cols), F32)
        ahead = dot_nt(rows, right[b, 0])
        for j in range(chunks):
            cross = ahead
            if j + 1 < chunks:
                ahead = dot_nt(rows, right[b, j + 1])
            values = jnp.exp(cross + col + sq_row[b, j, 0:1])
            high, low = split(values)
            total = total + (dot(high, vec[b, j]) + dot(low, vec[b, j]))
            if mirrored:
                acc_t[b, j] += dot(rows_vec, high) + dot(rows_vec, low)
        return fold(total.T)

    def self_step(c, carry):
        out_t[c] = tile(OWN, c, OWN, False)
        return carry

    lax.fori_loop(0, chunks, self_step, 0)

    mate_copy.wait_recv()

    def place_mate(c, carry):
        place_packed(MATE, c, mate_in)
        return carry

    lax.fori_loop(0, chunks, place_mate, 0)

    def step(k, carry):
        second = lax.rem(k, 2)
        c = jnp.where(even, lax.rem(k, chunks), lax.div(k, 2))
        uses_far = jnp.logical_or(odd == 1, k >= chunks)
        a = jnp.where(uses_far, FAR, MATE)
        b = jnp.where(even, OWN, jnp.where(second == 0, MATE, OWN))
        arrives = jnp.where(even, k >= chunks, second == 0)

        @pl.when(arrives)
        def _():
            far_copy(c).wait_recv()
            place_packed(FAR, c, far_in)

        part = tile(a, c, b, True)

        @pl.when(jnp.logical_not(uses_far))
        def _():
            mate_part[c] = part

        @pl.when(jnp.logical_and(uses_far, arrives))
        def _():
            far_part[c] = part

        @pl.when(jnp.logical_and(uses_far, jnp.logical_not(arrives)))
        def _():
            far_part[c] += part

        @pl.when(jnp.where(even, k >= chunks, second == 1))
        def _():
            part_copy(c).start()

        @pl.when(jnp.logical_and(even, k == chunks - 1))
        def _():
            mpart_copy.start()

        return carry

    lax.fori_loop(0, 2 * chunks, step, 0)

    @pl.when(odd == 1)
    def _():
        for c in range(chunks):
            mate_part[c] = fold(acc_t[MATE, c])
        mpart_copy.start()

    for c in range(chunks):
        out_t[c] += fold(acc_t[OWN, c])
    mpart_copy.wait_recv()
    for c in range(chunks):
        part_copy(c).wait_recv()
        o_ref[c * CHUNK : (c + 1) * CHUNK, :] = (out_t[c] + mate_back[c] + far_back[c]).T
    for c in range(chunks):
        far_copy(c).wait_send()
        part_copy(c).wait_send()
    mate_copy.wait_send()
    mpart_copy.wait_send()


def per_device(points, inv_scale, vectors):
    n = lax.axis_size(AXIS)
    rows, feat = points.shape
    cols = vectors.shape[1]
    chunks = rows // CHUNK
    packed = (chunks, CHUNK + 2 * cols, 128)
    turned = (chunks, cols, CHUNK)
    vmem = pl.BlockSpec(memory_space=pltpu.VMEM)
    sem = pltpu.SemaphoreType.DMA
    return pl.pallas_call(
        functools.partial(kernel, n),
        out_shape=jax.ShapeDtypeStruct((rows, cols), F32),
        in_specs=[vmem] * 3,
        out_specs=vmem,
        scratch_shapes=[
            pltpu.VMEM(packed, F32),
            pltpu.VMEM(packed, F32),
            pltpu.VMEM(packed, F32),
            pltpu.VMEM((3, chunks, CHUNK, 4 * feat), BF16),
            pltpu.VMEM((3, chunks, CHUNK, 4 * feat), BF16),
            pltpu.VMEM((3, chunks, CHUNK, 2 * cols), BF16),
            pltpu.VMEM((3, chunks, 2 * cols, CHUNK), BF16),
            pltpu.VMEM((3, chunks, CHUNK, 128), F32),
            pltpu.VMEM((3, chunks, 8, CHUNK), F32),
            pltpu.VMEM((2, chunks, 2 * cols, CHUNK), F32),
            pltpu.VMEM(turned, F32),
            pltpu.VMEM(turned, F32),
            pltpu.VMEM(turned, F32),
            pltpu.VMEM(turned, F32),
            pltpu.VMEM(turned, F32),
            sem((chunks,)), sem((chunks,)), sem, sem,
            sem((chunks,)), sem((chunks,)), sem, sem,
        ],
        compiler_params=pltpu.CompilerParams(
            collective_id=0, has_side_effects=True, vmem_limit_bytes=48 * 1024 * 1024
        ),
    )(points, inv_scale[None, :], vectors)


def solution(mesh):
    return jax.shard_map(
        per_device, mesh=mesh,
        in_specs=(P(AXIS, None), P(), P(AXIS, None)), out_specs=P(AXIS, None),
        check_vma=False,
    )
```

profile of v0, /device:TPU:1, one launch (start us, length us, event | category | flops | bytes accessed | tf_op | source)
XLA Modules:
  0.0 55.2 jit_solution(15173770828016328484)
XLA Ops:
  0.0 0.0 copy-start
  0.0 0.0 copy-start.1
  0.0 1.3 %copy.4.v_ref = f32[1536,64]{1,0:T(8,128)S(1)} copy(f32[1536,64]{0,1:T(8,128)} %param.5) | data formatting | bytes 786432 | tf_op args[2]
  1.3 0.0 copy-done
  1.4 0.0 copy-done.1
  1.4 52.8 %shard_map.37 = f32[1536,64]{1,0:T(8,128)S(1)} custom-call(f32[1536,128]{1,0:T(8,128)S(1)} %copy-done, f32[1,128]{1,0:T(1,128)S(1)} %bitcast.1, f32[1536,64]{1,0:T(8,128)S(1)} %copy.4.v_ref), custom_call_target="tpu_custom_call" | custom-call | tf_op jit(solution)/shard_map/pallas_call | solution.py:222
  54.2 1.0 %copy.5 = f32[1536,64]{0,1:T(8,128)} copy(f32[1536,64]{1,0:T(8,128)S(1)} %shard_map.37) | data formatting | bytes 786432 | tf_op jit(solution)/shard_map/pallas_call | solution.py:222
Async XLA Ops:
  0.0 1.3 %copy-start = (f32[1536,128]{1,0:T(8,128)S(1)}, f32[1536,128]{1,0:T(8,128)}, u32[]{:S(2)}) copy-start(f32[1536,128]{1,0:T(8,128)} %p_ref.1) | copy-start | bytes 2359300
  0.0 1.4 %copy-start.1 = (f32[128]{0:T(128)S(1)}, f32[128]{0:T(128)}, u32[]{:S(2)}) copy-start(f32[128]{0:T(128)} %param.4) | copy-start | bytes 1540
where the time goes:
time: 55.4 us; the launch traced here: 55.2 us
  Pallas kernels  52.8 us (95%)
  local copies, waits for them, and re-layouts  2.33 us (4%)
    pallas_call x1, Pallas kernels, per_device(): pl.pallas_call(functools.partial(kernel, n), out_shape=jax.ShapeDtypeStru...  52.8 us
    unnamed x5, local copies, waits for them, and re-layouts  1.34 us

commit v1 on v0

--- a/solution.py
+++ b/solution.py
@@ -8,7 +8,9 @@
 from jax.sharding import PartitionSpec as P
 
 AXIS = "blk"
-CHUNK = 256
+CHUNK = 512
+STRIP = 256
+LOG2E_ROOT = 1.2011224087864498
 OWN, MATE, FAR = 0, 1, 2
 MESH = pl.DeviceIdType.MESH
 F32, BF16 = jnp.float32, jnp.bfloat16
@@ -40,8 +42,8 @@
     part_send_sem, part_recv_sem, mpart_send_sem, mpart_recv_sem,
 ):
     chunks = p_ref.shape[0] // CHUNK
-    feat = p_ref.shape[1]
-    cols = v_ref.shape[1]
+    cols = v_ref.shape[0]
+    strips, lanes = CHUNK // STRIP, CHUNK // 128
     me = lax.axis_index(AXIS)
     odd = lax.rem(me, 2)
     even = odd == 0
@@ -57,42 +59,40 @@
     def place(slot, c, scaled, vt):
         high, low = split(scaled)
         left[slot, c] = jnp.concatenate([high, low, high, low], axis=1)
-        right[slot, c] = jnp.concatenate([high, low, low, high], axis=1)
+        turned = jnp.concatenate([high, low, low, high], axis=1)
         held = high.astype(F32) + low.astype(F32)
         squares = held * held
         sq_col[slot, c] = jnp.broadcast_to(
             -0.5 * jnp.sum(squares, axis=1, keepdims=True), (CHUNK, 128)
         )
-        sq_row[slot, c] = jnp.broadcast_to(
-            -0.5 * jnp.sum(squares.T, axis=0, keepdims=True), (8, CHUNK)
-        )
+        row = -0.5 * jnp.sum(squares.T, axis=0, keepdims=True)
         vt_high, vt_low = split(vt)
-        vec_t[slot, c] = jnp.concatenate([vt_high, vt_low], axis=0)
+        wide = jnp.concatenate([vt_high, vt_low], axis=0)
+        vec_t[slot, c] = jnp.concatenate([wide, wide], axis=1)
         v_high, v_low = split(vt.T)
-        vec[slot, c] = jnp.concatenate([v_high, v_low], axis=1)
+        tall = jnp.concatenate([v_high, v_low], axis=1)
+        for h in range(strips):
+            part = slice(h * STRIP, (h + 1) * STRIP)
+            j = c * strips + h
+            right[slot, j] = turned[part]
+            sq_row[slot, j] = jnp.broadcast_to(row[:, part], (8, STRIP))
+            vec[slot, j] = jnp.concatenate([tall[part], tall[part]], axis=0)
 
     def place_packed(slot, c, source):
-        scaled = source[c, :CHUNK]
-        vt = jnp.concatenate(
-            [source[c, CHUNK : CHUNK + cols], source[c, CHUNK + cols :]], axis=1
-        )
-        place(slot, c, scaled, vt)
-
-    scale = s_ref[...]
-
-    def prepare(c, carry):
+        pieces = [source[c, CHUNK + q * cols : CHUNK + (q + 1) * cols] for q in range(lanes)]
+        place(slot, c, source[c, :CHUNK], jnp.concatenate(pieces, axis=1))
+
+    scale = s_ref[...] * LOG2E_ROOT
+
+    def pack(c, carry):
         rows = pl.ds(pl.multiple_of(c * CHUNK, CHUNK), CHUNK)
-        scaled = p_ref[rows, :] * scale
-        vt = v_ref[rows, :].T
-        send[c, :CHUNK] = scaled
-        send[c, CHUNK : CHUNK + cols] = vt[:, :128]
-        send[c, CHUNK + cols :] = vt[:, 128:]
-        place(OWN, c, scaled, vt)
-        return carry
-
-    lax.fori_loop(0, chunks, prepare, 0)
-    acc_t[...] = jnp.zeros_like(acc_t)
-
+        send[c, :CHUNK] = p_ref[rows, :] * scale
+        vt = v_ref[:, rows]
+        for q in range(lanes):
+            send[c, CHUNK + q * cols : CHUNK + (q + 1) * cols] = vt[:, q * 128 : (q + 1) * 128]
+        return carry
+
+    lax.fori_loop(0, chunks, pack, 0)
     pl.semaphore_wait(barrier, 3)
 
     def far_copy(c):
@@ -121,21 +121,30 @@
         far_copy(c).start()
     mate_copy.start()
 
+    def place_own(c, carry):
+        place_packed(OWN, c, send)
+        return carry
+
+    lax.fori_loop(0, chunks, place_own, 0)
+    acc_t[...] = jnp.zeros_like(acc_t)
+
     def tile(a, c, b, mirrored):
         rows = left[a, c]
-        col = jnp.concatenate([sq_col[a, c]] * (CHUNK // 128), axis=1)
-        rows_vec = vec_t[a, c]
+        col = jnp.concatenate([sq_col[a, c]] * (STRIP // 128), axis=1)
+        count = chunks * strips
+        crosses, halves = {}, {}
         total = jnp.zeros((CHUNK, 2 * cols), F32)
-        ahead = dot_nt(rows, right[b, 0])
-        for j in range(chunks):
-            cross = ahead
-            if j + 1 < chunks:
-                ahead = dot_nt(rows, right[b, j + 1])
-            values = jnp.exp(cross + col + sq_row[b, j, 0:1])
-            high, low = split(values)
-            total = total + (dot(high, vec[b, j]) + dot(low, vec[b, j]))
-            if mirrored:
-                acc_t[b, j] += dot(rows_vec, high) + dot(rows_vec, low)
+        for j in range(count + 2):
+            if j < count:
+                crosses[j] = dot_nt(rows, right[b, j])
+            if 2 <= j:
+                high, low = halves.pop(j - 2)
+                total = total + dot(jnp.concatenate([high, low], axis=1), vec[b, j - 2])
+                if mirrored:
+                    acc_t[b, j - 2] += dot(vec_t[a, c], jnp.concatenate([high, low], axis=0))
+            if 1 <= j <= count:
+                cross = crosses.pop(j - 1)
+                halves[j - 1] = split(jnp.exp2(cross + col + sq_row[b, j - 1, 0:1]))
         return fold(total.T)
 
     def self_step(c, carry):
@@ -191,18 +200,22 @@
 
     lax.fori_loop(0, 2 * chunks, step, 0)
 
+    def mirror_of(b, c):
+        pieces = [fold(acc_t[b, c * strips + h]) for h in range(strips)]
+        return jnp.concatenate(pieces, axis=1)
+
     @pl.when(odd == 1)
     def _():
         for c in range(chunks):
-            mate_part[c] = fold(acc_t[MATE, c])
+            mate_part[c] = mirror_of(MATE, c)
         mpart_copy.start()
 
     for c in range(chunks):
-        out_t[c] += fold(acc_t[OWN, c])
+        out_t[c] += mirror_of(OWN, c)
     mpart_copy.wait_recv()
     for c in range(chunks):
         part_copy(c).wait_recv()
-        o_ref[c * CHUNK : (c + 1) * CHUNK, :] = (out_t[c] + mate_back[c] + far_back[c]).T
+        o_ref[:, c * CHUNK : (c + 1) * CHUNK] = out_t[c] + mate_back[c] + far_back[c]
     for c in range(chunks):
         far_copy(c).wait_send()
         part_copy(c).wait_send()
@@ -215,13 +228,14 @@
     rows, feat = points.shape
     cols = vectors.shape[1]
     chunks = rows // CHUNK
-    packed = (chunks, CHUNK + 2 * cols, 128)
+    strips = rows // STRIP
+    packed = (chunks, CHUNK + CHUNK // 128 * cols, 128)
     turned = (chunks, cols, CHUNK)
     vmem = pl.BlockSpec(memory_space=pltpu.VMEM)
     sem = pltpu.SemaphoreType.DMA
     return pl.pallas_call(
         functools.partial(kernel, n),
-        out_shape=jax.ShapeDtypeStruct((rows, cols), F32),
+        out_shape=jax.ShapeDtypeStruct((cols, rows), F32),
         in_specs=[vmem] * 3,
         out_specs=vmem,
         scratch_shapes=[
@@ -229,12 +243,12 @@
             pltpu.VMEM(packed, F32),
             pltpu.VMEM(packed, F32),
             pltpu.VMEM((3, chunks, CHUNK, 4 * feat), BF16),
-            pltpu.VMEM((3, chunks, CHUNK, 4 * feat), BF16),
-            pltpu.VMEM((3, chunks, CHUNK, 2 * cols), BF16),
-            pltpu.VMEM((3, chunks, 2 * cols, CHUNK), BF16),
+            pltpu.VMEM((3, strips, STRIP, 4 * feat), BF16),
+            pltpu.VMEM((3, strips, 2 * STRIP, 2 * cols), BF16),
+            pltpu.VMEM((3, chunks, 2 * cols, 2 * CHUNK), BF16),
             pltpu.VMEM((3, chunks, CHUNK, 128), F32),
-            pltpu.VMEM((3, chunks, 8, CHUNK), F32),
-            pltpu.VMEM((2, chunks, 2 * cols, CHUNK), F32),
+            pltpu.VMEM((3, strips, 8, STRIP), F32),
+            pltpu.VMEM((2, strips, 2 * cols, STRIP), F32),
             pltpu.VMEM(turned, F32),
             pltpu.VMEM(turned, F32),
             pltpu.VMEM(turned, F32),
@@ -246,7 +260,7 @@
         compiler_params=pltpu.CompilerParams(
             collective_id=0, has_side_effects=True, vmem_limit_bytes=48 * 1024 * 1024
         ),
-    )(points, inv_scale[None, :], vectors)
+    )(points, inv_scale[None, :], vectors.T).T
 
 
 def solution(mesh):

time: 55.4 us -> 54.7 us (0.987)
  Pallas kernels: 52.8 us -> 50.9 us
  local copies, waits for them, and re-layouts: 2.33 us -> 3.53 us
    unnamed x5 -> x7, local copies, waits for them, and re-layouts: 1.34 us -> 3.53 us
    pallas_call x1, Pallas kernels: 52.8 us -> 50.9 us  [per_device(): pl.pallas_call(functools.partial(kernel, n), out_shape=jax.ShapeDtypeStru...]
    pallas_call x1 -> x0, local copies, waits for them, and re-layouts: 1 us -> none  [per_device(): pl.pallas_call(functools.partial(kernel, n), out_shape=jax.ShapeDtypeStru...]
where the time goes in v1:
time: 54.7 us; the launch traced here: 54.5 us
  Pallas kernels  50.9 us (93%)
  local copies, waits for them, and re-layouts  3.53 us (6%)
    pallas_call x1, Pallas kernels, per_device(): pl.pallas_call(functools.partial(kernel, n), out_shape=jax.ShapeDtypeStru...  50.9 us
    unnamed x7, local copies, waits for them, and re-layouts  3.53 us

profile of v1, /device:TPU:1, one launch (start us, length us, event | category | flops | bytes accessed | tf_op | source)
XLA Modules:
  0.0 54.5 jit_solution(8010759776848133856)
XLA Ops:
  0.0 0.0 copy-start.2
  0.0 0.7 %copy-done.2 = f32[128]{0:T(128)S(1)} copy-done((f32[128]{0:T(128)S(1)}, f32[128]{0:T(128)}, u32[]{:S(2)}) %copy-start.2) | copy-done | bytes 536
  0.7 0.0 copy-start
  0.7 1.1 %copy-done = f32[1536,128]{1,0:T(8,128)S(1)} copy-done((f32[1536,128]{1,0:T(8,128)S(1)}, f32[1536,128]{1,0:T(8,128)}, u32[]{:S(2)}) %copy-start) | copy-done | bytes 786456
  1.8 0.0 copy-start.1
  1.8 1.0 %copy-done.1 = f32[1536,64]{0,1:T(8,128)S(1)} copy-done((f32[1536,64]{0,1:T(8,128)S(1)}, f32[1536,64]{0,1:T(8,128)}, u32[]{:S(2)}) %copy-start.1) | copy-done | bytes 393240
  2.8 50.9 %shard_map.37 = f32[64,1536]{1,0:T(8,128)S(1)} custom-call(f32[1536,128]{1,0:T(8,128)S(1)} %copy-done, f32[1,128]{1,0:T(1,128)S(1)} %bitcast.5, f32[64,1536]{1,0:T(8,128)S(1)} %bitcast.4), custom_call_target="tpu_custom_call" | custom-call | tf_op jit(solution)/shard_map/pallas_call | solution.py:236
  53.7 0.7 %copy.5 = f32[1536,64]{0,1:T(8,128)} copy(f32[1536,64]{0,1:T(8,128)S(1)} %bitcast.3) | data formatting | bytes 786432
Async XLA Ops:
  0.0 0.7 %copy-start.2 = (f32[128]{0:T(128)S(1)}, f32[128]{0:T(128)}, u32[]{:S(2)}) copy-start(f32[128]{0:T(128)} %param.4) | copy-start | bytes 1540
  0.7 1.1 %copy-start = (f32[1536,128]{1,0:T(8,128)S(1)}, f32[1536,128]{1,0:T(8,128)}, u32[]{:S(2)}) copy-start(f32[1536,128]{1,0:T(8,128)} %p_ref.1) | copy-start | bytes 2359300
  1.8 1.0 %copy-start.1 = (f32[1536,64]{0,1:T(8,128)S(1)}, f32[1536,64]{0,1:T(8,128)}, u32[]{:S(2)}) copy-start(f32[1536,64]{0,1:T(8,128)} %param.5) | copy-start | bytes 1179652

commit v2 on v1

--- a/solution.py
+++ b/solution.py
@@ -36,7 +36,7 @@
 
 def kernel(
     n, p_ref, s_ref, v_ref, o_ref,
-    send, far_in, mate_in, left, right, vec, vec_t, sq_col, sq_row, acc_t, out_t,
+    send, far_in, mate_in, left, right, vec, sq_col, sq_row, acc_t, out_t,
     far_part, mate_part, far_back, mate_back,
     far_send_sem, far_recv_sem, mate_send_sem, mate_recv_sem,
     part_send_sem, part_recv_sem, mpart_send_sem, mpart_recv_sem,
@@ -53,7 +53,7 @@
     guest = jnp.where(even, up, down)
 
     barrier = pltpu.get_barrier_semaphore()
-    for other in (mate, up, down):
+    for other in (mate, guest):
         pl.semaphore_signal(barrier, inc=1, device_id=(other,), device_id_type=MESH)
 
     def place(slot, c, scaled, vt):
@@ -66,9 +66,6 @@
             -0.5 * jnp.sum(squares, axis=1, keepdims=True), (CHUNK, 128)
         )
         row = -0.5 * jnp.sum(squares.T, axis=0, keepdims=True)
-        vt_high, vt_low = split(vt)
-        wide = jnp.concatenate([vt_high, vt_low], axis=0)
-        vec_t[slot, c] = jnp.concatenate([wide, wide], axis=1)
         v_high, v_low = split(vt.T)
         tall = jnp.concatenate([v_high, v_low], axis=1)
         for h in range(strips):
@@ -93,7 +90,7 @@
         return carry
 
     lax.fori_loop(0, chunks, pack, 0)
-    pl.semaphore_wait(barrier, 3)
+    pl.semaphore_wait(barrier, 2)
 
     def far_copy(c):
         return pltpu.make_async_remote_copy(
@@ -117,8 +114,11 @@
         src_ref=mate_part, dst_ref=mate_back, send_sem=mpart_send_sem,
         recv_sem=mpart_recv_sem, device_id=(mate,), device_id_type=MESH,
     )
-    for c in range(chunks):
-        far_copy(c).start()
+    @pl.when(odd == 1)
+    def _():
+        for c in range(chunks):
+            far_copy(c).start()
+
     mate_copy.start()
 
     def place_own(c, carry):
@@ -141,7 +141,12 @@
                 high, low = halves.pop(j - 2)
                 total = total + dot(jnp.concatenate([high, low], axis=1), vec[b, j - 2])
                 if mirrored:
-                    acc_t[b, j - 2] += dot(vec_t[a, c], jnp.concatenate([high, low], axis=0))
+                    turned = []
+                    for h in range(strips):
+                        part = slice(h * STRIP, (h + 1) * STRIP)
+                        turned += [high[part].T, low[part].T]
+                    weights = jnp.concatenate([vec[a, c * strips + h] for h in range(strips)], axis=0)
+                    acc_t[b, j - 2] += dot(jnp.concatenate(turned, axis=1), weights)
             if 1 <= j <= count:
                 cross = crosses.pop(j - 1)
                 halves[j - 1] = split(jnp.exp2(cross + col + sq_row[b, j - 1, 0:1]))
@@ -149,6 +154,11 @@
 
     def self_step(c, carry):
         out_t[c] = tile(OWN, c, OWN, False)
+
+        @pl.when(even)
+        def _():
+            far_copy(c).start()
+
         return carry
 
     lax.fori_loop(0, chunks, self_step, 0)
@@ -201,7 +211,7 @@
     lax.fori_loop(0, 2 * chunks, step, 0)
 
     def mirror_of(b, c):
-        pieces = [fold(acc_t[b, c * strips + h]) for h in range(strips)]
+        pieces = [fold(acc_t[b, c * strips + h].T) for h in range(strips)]
         return jnp.concatenate(pieces, axis=1)
 
     @pl.when(odd == 1)
@@ -245,10 +255,9 @@
             pltpu.VMEM((3, chunks, CHUNK, 4 * feat), BF16),
             pltpu.VMEM((3, strips, STRIP, 4 * feat), BF16),
             pltpu.VMEM((3, strips, 2 * STRIP, 2 * cols), BF16),
-            pltpu.VMEM((3, chunks, 2 * cols, 2 * CHUNK), BF16),
             pltpu.VMEM((3, chunks, CHUNK, 128), F32),
             pltpu.VMEM((3, strips, 8, STRIP), F32),
-            pltpu.VMEM((2, strips, 2 * cols, STRIP), F32),
+            pltpu.VMEM((2, strips, STRIP, 2 * cols), F32),
             pltpu.VMEM(turned, F32),
             pltpu.VMEM(turned, F32),
             pltpu.VMEM(turned, F32),

time: 54.7 us -> 49.1 us (0.90)
  Pallas kernels: 50.9 us -> 45.4 us
    pallas_call x1, Pallas kernels: 50.9 us -> 45.4 us  [per_device(): pl.pallas_call(functools.partial(kernel, n), out_shape=jax.ShapeDtypeStru...]
where the time goes in v2:
time: 49.1 us; the launch traced here: 48.9 us
  Pallas kernels  45.4 us (92%)
  local copies, waits for them, and re-layouts  3.53 us (7%)
    pallas_call x1, Pallas kernels, per_device(): pl.pallas_call(functools.partial(kernel, n), out_shape=jax.ShapeDtypeStru...  45.4 us
    unnamed x7, local copies, waits for them, and re-layouts  3.53 us

profile of v2, /device:TPU:1, one launch (start us, length us, event | category | flops | bytes accessed | tf_op | source)
XLA Modules:
  0.0 48.9 jit_solution(10783224059266950375)
XLA Ops:
  0.0 0.0 copy-start.2
  0.0 0.7 %copy-done.2 = f32[128]{0:T(128)S(1)} copy-done((f32[128]{0:T(128)S(1)}, f32[128]{0:T(128)}, u32[]{:S(2)}) %copy-start.2) | copy-done | bytes 536
  0.7 0.0 copy-start
  0.7 1.1 %copy-done = f32[1536,128]{1,0:T(8,128)S(1)} copy-done((f32[1536,128]{1,0:T(8,128)S(1)}, f32[1536,128]{1,0:T(8,128)}, u32[]{:S(2)}) %copy-start) | copy-done | bytes 786456
  1.8 0.0 copy-start.1
  1.8 1.0 %copy-done.1 = f32[1536,64]{0,1:T(8,128)S(1)} copy-done((f32[1536,64]{0,1:T(8,128)S(1)}, f32[1536,64]{0,1:T(8,128)}, u32[]{:S(2)}) %copy-start.1) | copy-done | bytes 393240
  2.8 45.4 %shard_map.37 = f32[64,1536]{1,0:T(8,128)S(1)} custom-call(f32[1536,128]{1,0:T(8,128)S(1)} %copy-done, f32[1,128]{1,0:T(1,128)S(1)} %bitcast.5, f32[64,1536]{1,0:T(8,128)S(1)} %bitcast.4), custom_call_target="tpu_custom_call" | custom-call | tf_op jit(solution)/shard_map/pallas_call | solution.py:246
  48.1 0.7 %copy.5 = f32[1536,64]{0,1:T(8,128)} copy(f32[1536,64]{0,1:T(8,128)S(1)} %bitcast.3) | data formatting | bytes 786432
Async XLA Ops:
  0.0 0.7 %copy-start.2 = (f32[128]{0:T(128)S(1)}, f32[128]{0:T(128)}, u32[]{:S(2)}) copy-start(f32[128]{0:T(128)} %param.4) | copy-start | bytes 1540
  0.7 1.1 %copy-start = (f32[1536,128]{1,0:T(8,128)S(1)}, f32[1536,128]{1,0:T(8,128)}, u32[]{:S(2)}) copy-start(f32[1536,128]{1,0:T(8,128)} %p_ref.1) | copy-start | bytes 2359300
  1.8 1.0 %copy-start.1 = (f32[1536,64]{0,1:T(8,128)S(1)}, f32[1536,64]{0,1:T(8,128)}, u32[]{:S(2)}) copy-start(f32[1536,64]{0,1:T(8,128)} %param.5) | copy-start | bytes 1179652

commit v3 on v2

--- a/solution.py
+++ b/solution.py
@@ -36,9 +36,10 @@
 
 def kernel(
     n, p_ref, s_ref, v_ref, o_ref,
-    send, far_in, mate_in, left, right, vec, sq_col, sq_row, acc_t, out_t,
+    send, far_in, mate_in, left, right, vec, vec_t, sq_col, sq_row, acc_t, out_t,
+    cross, tile_high, tile_low, scale_in,
     far_part, mate_part, far_back, mate_back,
-    far_send_sem, far_recv_sem, mate_send_sem, mate_recv_sem,
+    load_sem, scale_sem, far_send_sem, far_recv_sem, mate_send_sem, mate_recv_sem,
     part_send_sem, part_recv_sem, mpart_send_sem, mpart_recv_sem,
 ):
     chunks = p_ref.shape[0] // CHUNK
@@ -53,43 +54,50 @@
     guest = jnp.where(even, up, down)
 
     barrier = pltpu.get_barrier_semaphore()
+
+    def load_parts(c):
+        pairs = [(p_ref.at[c * CHUNK : (c + 1) * CHUNK], send.at[c, 0:CHUNK])]
+        for q in range(lanes):
+            first = c * CHUNK + q * 128
+            at = CHUNK + q * cols
+            pairs.append((v_ref.at[:, first : first + 128], send.at[c, at : at + cols]))
+        return [
+            pltpu.make_async_copy(src, dst, load_sem.at[c, i])
+            for i, (src, dst) in enumerate(pairs)
+        ]
+
+    loads = [load_parts(c) for c in range(chunks)]
+    scale_load = pltpu.make_async_copy(s_ref, scale_in, scale_sem)
+    scale_load.start()
+    for group in loads:
+        for copy in group:
+            copy.start()
     for other in (mate, guest):
         pl.semaphore_signal(barrier, inc=1, device_id=(other,), device_id_type=MESH)
 
-    def place(slot, c, scaled, vt):
-        high, low = split(scaled)
+    def place(slot, c, source):
+        rows = pl.ds(pl.multiple_of(c * CHUNK, CHUNK), CHUNK)
+        pieces = [source[c, CHUNK + q * cols : CHUNK + (q + 1) * cols] for q in range(lanes)]
+        high, low = split(source[c, :CHUNK])
         left[slot, c] = jnp.concatenate([high, low, high, low], axis=1)
-        turned = jnp.concatenate([high, low, low, high], axis=1)
+        right[slot, rows] = jnp.concatenate([high, low, low, high], axis=1)
         held = high.astype(F32) + low.astype(F32)
         squares = held * held
         sq_col[slot, c] = jnp.broadcast_to(
             -0.5 * jnp.sum(squares, axis=1, keepdims=True), (CHUNK, 128)
         )
         row = -0.5 * jnp.sum(squares.T, axis=0, keepdims=True)
-        v_high, v_low = split(vt.T)
-        tall = jnp.concatenate([v_high, v_low], axis=1)
-        for h in range(strips):
-            part = slice(h * STRIP, (h + 1) * STRIP)
-            j = c * strips + h
-            right[slot, j] = turned[part]
-            sq_row[slot, j] = jnp.broadcast_to(row[:, part], (8, STRIP))
-            vec[slot, j] = jnp.concatenate([tall[part], tall[part]], axis=0)
-
-    def place_packed(slot, c, source):
-        pieces = [source[c, CHUNK + q * cols : CHUNK + (q + 1) * cols] for q in range(lanes)]
-        place(slot, c, source[c, :CHUNK], jnp.concatenate(pieces, axis=1))
-
-    scale = s_ref[...] * LOG2E_ROOT
-
-    def pack(c, carry):
-        rows = pl.ds(pl.multiple_of(c * CHUNK, CHUNK), CHUNK)
-        send[c, :CHUNK] = p_ref[rows, :] * scale
-        vt = v_ref[:, rows]
-        for q in range(lanes):
-            send[c, CHUNK + q * cols : CHUNK + (q + 1) * cols] = vt[:, q * 128 : (q + 1) * 128]
-        return carry
-
-    lax.fori_loop(0, chunks, pack, 0)
+        sq_row[slot, :, rows] = jnp.broadcast_to(row, (8, CHUNK))
+        vt = jnp.concatenate(pieces, axis=1)
+        vec_t[slot, c] = jnp.concatenate(split(vt), axis=0)
+        vec[slot, rows] = jnp.concatenate(split(vt.T), axis=1)
+
+    scale_load.wait()
+    scale = scale_in[...] * LOG2E_ROOT
+    for c in range(chunks):
+        for copy in loads[c]:
+            copy.wait()
+        send[c, :CHUNK] = send[c, :CHUNK] * scale
     pl.semaphore_wait(barrier, 2)
 
     def far_copy(c):
@@ -122,34 +130,22 @@
     mate_copy.start()
 
     def place_own(c, carry):
-        place_packed(OWN, c, send)
+        place(OWN, c, send)
         return carry
 
     lax.fori_loop(0, chunks, place_own, 0)
     acc_t[...] = jnp.zeros_like(acc_t)
 
     def tile(a, c, b, mirrored):
-        rows = left[a, c]
         col = jnp.concatenate([sq_col[a, c]] * (STRIP // 128), axis=1)
-        count = chunks * strips
-        crosses, halves = {}, {}
-        total = jnp.zeros((CHUNK, 2 * cols), F32)
-        for j in range(count + 2):
-            if j < count:
-                crosses[j] = dot_nt(rows, right[b, j])
-            if 2 <= j:
-                high, low = halves.pop(j - 2)
-                total = total + dot(jnp.concatenate([high, low], axis=1), vec[b, j - 2])
-                if mirrored:
-                    turned = []
-                    for h in range(strips):
-                        part = slice(h * STRIP, (h + 1) * STRIP)
-                        turned += [high[part].T, low[part].T]
-                    weights = jnp.concatenate([vec[a, c * strips + h] for h in range(strips)], axis=0)
-                    acc_t[b, j - 2] += dot(jnp.concatenate(turned, axis=1), weights)
-            if 1 <= j <= count:
-                cross = crosses.pop(j - 1)
-                halves[j - 1] = split(jnp.exp2(cross + col + sq_row[b, j - 1, 0:1]))
+        cross[...] = dot_nt(left[a, c], right[b])
+        for j in range(chunks * strips):
+            at = slice(j * STRIP, (j + 1) * STRIP)
+            values = jnp.exp2(cross[:, at] + col + sq_row[b, 0:1, at])
+            tile_high[:, at], tile_low[:, at] = split(values)
+        total = dot(tile_high[...], vec[b]) + dot(tile_low[...], vec[b])
+        if mirrored:
+            acc_t[b] += dot(vec_t[a, c], tile_high[...]) + dot(vec_t[a, c], tile_low[...])
         return fold(total.T)
 
     def self_step(c, carry):
@@ -166,7 +162,7 @@
     mate_copy.wait_recv()
 
     def place_mate(c, carry):
-        place_packed(MATE, c, mate_in)
+        place(MATE, c, mate_in)
         return carry
 
     lax.fori_loop(0, chunks, place_mate, 0)
@@ -182,7 +178,7 @@
         @pl.when(arrives)
         def _():
             far_copy(c).wait_recv()
-            place_packed(FAR, c, far_in)
+            place(FAR, c, far_in)
 
         part = tile(a, c, b, True)
 
@@ -211,8 +207,7 @@
     lax.fori_loop(0, 2 * chunks, step, 0)
 
     def mirror_of(b, c):
-        pieces = [fold(acc_t[b, c * strips + h].T) for h in range(strips)]
-        return jnp.concatenate(pieces, axis=1)
+        return fold(acc_t[b, :, c * CHUNK : (c + 1) * CHUNK])
 
     @pl.when(odd == 1)
     def _():
@@ -238,7 +233,6 @@
     rows, feat = points.shape
     cols = vectors.shape[1]
     chunks = rows // CHUNK
-    strips = rows // STRIP
     packed = (chunks, CHUNK + CHUNK // 128 * cols, 128)
     turned = (chunks, cols, CHUNK)
     vmem = pl.BlockSpec(memory_space=pltpu.VMEM)
@@ -246,23 +240,29 @@
     return pl.pallas_call(
         functools.partial(kernel, n),
         out_shape=jax.ShapeDtypeStruct((cols, rows), F32),
-        in_specs=[vmem] * 3,
+        in_specs=[pl.BlockSpec(memory_space=pl.ANY)] * 3,
         out_specs=vmem,
         scratch_shapes=[
             pltpu.VMEM(packed, F32),
             pltpu.VMEM(packed, F32),
             pltpu.VMEM(packed, F32),
             pltpu.VMEM((3, chunks, CHUNK, 4 * feat), BF16),
-            pltpu.VMEM((3, strips, STRIP, 4 * feat), BF16),
-            pltpu.VMEM((3, strips, 2 * STRIP, 2 * cols), BF16),
+            pltpu.VMEM((3, rows, 4 * feat), BF16),
+            pltpu.VMEM((3, rows, 2 * cols), BF16),
+            pltpu.VMEM((3, chunks, 2 * cols, CHUNK), BF16),
             pltpu.VMEM((3, chunks, CHUNK, 128), F32),
-            pltpu.VMEM((3, strips, 8, STRIP), F32),
-            pltpu.VMEM((2, strips, STRIP, 2 * cols), F32),
-            pltpu.VMEM(turned, F32),
-            pltpu.VMEM(turned, F32),
-            pltpu.VMEM(turned, F32),
-            pltpu.VMEM(turned, F32),
-            pltpu.VMEM(turned, F32),
+            pltpu.VMEM((3, 8, rows), F32),
+            pltpu.VMEM((2, 2 * cols, rows), F32),
+            pltpu.VMEM(turned, F32),
+            pltpu.VMEM((CHUNK, rows), F32),
+            pltpu.VMEM((CHUNK, rows), BF16),
+            pltpu.VMEM((CHUNK, rows), BF16),
+            pltpu.VMEM((1, feat), F32),
+            pltpu.VMEM(turned, F32),
+            pltpu.VMEM(turned, F32),
+            pltpu.VMEM(turned, F32),
+            pltpu.VMEM(turned, F32),
+            sem((chunks, 1 + CHUNK // 128)), sem,
             sem((chunks,)), sem((chunks,)), sem, sem,
             sem((chunks,)), sem((chunks,)), sem, sem,
         ],

time: 49.1 us -> 50.1 us (1.020)
  the two profiles are of different devices: /device:TPU:1 before, /device:TPU:6 now
where the time goes in v3:
time: 50.1 us; the launch traced here: 49.9 us
  Pallas kernels  46.3 us (92%)
  local copies, waits for them, and re-layouts  3.53 us (7%)
    pallas_call x1, Pallas kernels, per_device(): pl.pallas_call(functools.partial(kernel, n), out_shape=jax.ShapeDtypeStru...  46.3 us
    unnamed x7, local copies, waits for them, and re-layouts  3.53 us

profile of v3, /device:TPU:6, one launch (start us, length us, event | category | flops | bytes accessed | tf_op | source)
XLA Modules:
  0.0 49.9 jit_solution(9457565094796320593)
XLA Ops:
  0.0 0.0 copy-start.2
  0.0 0.7 %copy-done.2 = f32[128]{0:T(128)S(1)} copy-done((f32[128]{0:T(128)S(1)}, f32[128]{0:T(128)}, u32[]{:S(2)}) %copy-start.2) | copy-done | bytes 536
  0.7 0.0 copy-start
  0.7 1.1 %copy-done = f32[1536,128]{1,0:T(8,128)S(1)} copy-done((f32[1536,128]{1,0:T(8,128)S(1)}, f32[1536,128]{1,0:T(8,128)}, u32[]{:S(2)}) %copy-start) | copy-done | bytes 786456
  1.8 0.0 copy-start.1
  1.8 1.0 %copy-done.1 = f32[1536,64]{0,1:T(8,128)S(1)} copy-done((f32[1536,64]{0,1:T(8,128)S(1)}, f32[1536,64]{0,1:T(8,128)}, u32[]{:S(2)}) %copy-start.1) | copy-done | bytes 393240
  2.8 46.3 %shard_map.37 = f32[64,1536]{1,0:T(8,128)S(1)} custom-call(f32[1536,128]{1,0:T(8,128)S(1)} %copy-done, f32[1,128]{1,0:T(1,128)S(1)} %bitcast.5, f32[64,1536]{1,0:T(8,128)S(1)} %bitcast.4), custom_call_target="tpu_custom_call" | custom-call | tf_op jit(solution)/shard_map/pallas_call | solution.py:240
  49.1 0.7 %copy.5 = f32[1536,64]{0,1:T(8,128)} copy(f32[1536,64]{0,1:T(8,128)S(1)} %bitcast.3) | data formatting | bytes 786432
Async XLA Ops:
  0.0 0.7 %copy-start.2 = (f32[128]{0:T(128)S(1)}, f32[128]{0:T(128)}, u32[]{:S(2)}) copy-start(f32[128]{0:T(128)} %param.4) | copy-start | bytes 1540
  0.7 1.1 %copy-start = (f32[1536,128]{1,0:T(8,128)S(1)}, f32[1536,128]{1,0:T(8,128)}, u32[]{:S(2)}) copy-start(f32[1536,128]{1,0:T(8,128)} %p_ref.1) | copy-start | bytes 2359300
  1.8 1.0 %copy-start.1 = (f32[1536,64]{0,1:T(8,128)S(1)}, f32[1536,64]{0,1:T(8,128)}, u32[]{:S(2)}) copy-start(f32[1536,64]{0,1:T(8,128)} %param.5) | copy-start | bytes 1179652

commit v4 on v3

--- a/solution.py
+++ b/solution.py
@@ -36,10 +36,10 @@
 
 def kernel(
     n, p_ref, s_ref, v_ref, o_ref,
-    send, far_in, mate_in, left, right, vec, vec_t, sq_col, sq_row, acc_t, out_t,
+    send, far_in, mate_in, relay_in, left, right, vec, vec_t, sq_col, sq_row, acc_t, out_t,
     cross, tile_high, tile_low, scale_in,
     far_part, mate_part, far_back, mate_back,
-    load_sem, scale_sem, far_send_sem, far_recv_sem, mate_send_sem, mate_recv_sem,
+    load_sem, scale_sem, far_send_sem, far_recv_sem, relay_send_sem, relay_recv_sem, mate_send_sem, mate_recv_sem,
     part_send_sem, part_recv_sem, mpart_send_sem, mpart_recv_sem,
 ):
     chunks = p_ref.shape[0] // CHUNK
@@ -53,6 +53,15 @@
     host = jnp.where(even, down, up)
     guest = jnp.where(even, up, down)
 
+    even_i = 1 - odd
+    place_in = lax.rem(me, 8)
+    relayed = n % 8 == 0
+    source = jnp.logical_and(relayed, jnp.logical_or(place_in == 3, place_in == 4))
+    relay = jnp.logical_and(relayed, jnp.logical_or(place_in == 1, place_in == 6))
+    target = jnp.logical_and(relayed, jnp.logical_or(place_in == 2, place_in == 5))
+    host_two = lax.rem(me + 4 * odd + (n - 4) * even_i, n)
+    guest_two = lax.rem(me + 4 * even_i + (n - 4) * odd, n)
+
     barrier = pltpu.get_barrier_semaphore()
 
     def load_parts(c):
@@ -72,8 +81,13 @@
     for group in loads:
         for copy in group:
             copy.start()
-    for other in (mate, guest):
+    first_sender = jnp.where(target, guest_two, guest)
+    for other in (mate, first_sender):
         pl.semaphore_signal(barrier, inc=1, device_id=(other,), device_id_type=MESH)
+
+    @pl.when(relay)
+    def _():
+        pl.semaphore_signal(barrier, inc=1, device_id=(host,), device_id_type=MESH)
 
     def place(slot, c, source):
         rows = pl.ds(pl.multiple_of(c * CHUNK, CHUNK), CHUNK)
@@ -98,7 +112,7 @@
         for copy in loads[c]:
             copy.wait()
         send[c, :CHUNK] = send[c, :CHUNK] * scale
-    pl.semaphore_wait(barrier, 2)
+    pl.semaphore_wait(barrier, 2 + relay.astype(jnp.int32))
 
     def far_copy(c):
         return pltpu.make_async_remote_copy(
@@ -106,6 +120,33 @@
             send_sem=far_send_sem.at[c], recv_sem=far_recv_sem.at[c],
             device_id=(host,), device_id_type=MESH,
         )
+
+    def source_copy(c):
+        return pltpu.make_async_remote_copy(
+            src_ref=send.at[c], dst_ref=relay_in.at[c],
+            send_sem=far_send_sem.at[c], recv_sem=relay_recv_sem.at[c],
+            device_id=(guest,), device_id_type=MESH,
+        )
+
+    def relay_copy(c):
+        return pltpu.make_async_remote_copy(
+            src_ref=relay_in.at[c], dst_ref=far_in.at[c],
+            send_sem=relay_send_sem.at[c], recv_sem=far_recv_sem.at[c],
+            device_id=(host_two,), device_id_type=MESH,
+        )
+
+    def send_far(c):
+        @pl.when(source)
+        def _():
+            source_copy(c).start()
+
+        @pl.when(jnp.logical_not(source))
+        def _():
+            far_copy(c).start()
+
+    def pass_on(c):
+        source_copy(c).wait_recv()
+        relay_copy(c).start()
 
     def part_copy(c):
         return pltpu.make_async_remote_copy(
@@ -125,7 +166,7 @@
     @pl.when(odd == 1)
     def _():
         for c in range(chunks):
-            far_copy(c).start()
+            send_far(c)
 
     mate_copy.start()
 
@@ -136,28 +177,38 @@
     lax.fori_loop(0, chunks, place_own, 0)
     acc_t[...] = jnp.zeros_like(acc_t)
 
-    def tile(a, c, b, mirrored):
+    def fill(a, c, b, first):
         col = jnp.concatenate([sq_col[a, c]] * (STRIP // 128), axis=1)
-        cross[...] = dot_nt(left[a, c], right[b])
-        for j in range(chunks * strips):
-            at = slice(j * STRIP, (j + 1) * STRIP)
+        cross[:, first:] = dot_nt(left[a, c], right[b, first:])
+        for start in range(first, chunks * CHUNK, STRIP):
+            at = slice(start, start + STRIP)
             values = jnp.exp2(cross[:, at] + col + sq_row[b, 0:1, at])
             tile_high[:, at], tile_low[:, at] = split(values)
-        total = dot(tile_high[...], vec[b]) + dot(tile_low[...], vec[b])
-        if mirrored:
-            acc_t[b] += dot(vec_t[a, c], tile_high[...]) + dot(vec_t[a, c], tile_low[...])
+        total = dot(tile_high[:, first:], vec[b, first:]) + dot(tile_low[:, first:], vec[b, first:])
         return fold(total.T)
 
-    def self_step(c, carry):
-        out_t[c] = tile(OWN, c, OWN, False)
+    def mirror(a, c, b, first):
+        acc_t[b, :, first:] += dot(vec_t[a, c], tile_high[:, first:]) + dot(
+            vec_t[a, c], tile_low[:, first:]
+        )
+
+    def tile(a, c, b):
+        part = fill(a, c, b, 0)
+        mirror(a, c, b, 0)
+        return part
+
+    for c in range(chunks):
+        out_t[c] = fill(OWN, c, OWN, c * CHUNK)
+        if c + 1 < chunks:
+            mirror(OWN, c, OWN, (c + 1) * CHUNK)
 
         @pl.when(even)
         def _():
-            far_copy(c).start()
-
-        return carry
-
-    lax.fori_loop(0, chunks, self_step, 0)
+            send_far(c)
+
+        @pl.when(jnp.logical_and(relay, odd == 1))
+        def _():
+            pass_on(c)
 
     mate_copy.wait_recv()
 
@@ -180,7 +231,7 @@
             far_copy(c).wait_recv()
             place(FAR, c, far_in)
 
-        part = tile(a, c, b, True)
+        part = tile(a, c, b)
 
         @pl.when(jnp.logical_not(uses_far))
         def _():
@@ -197,6 +248,10 @@
         @pl.when(jnp.where(even, k >= chunks, second == 1))
         def _():
             part_copy(c).start()
+
+        @pl.when(jnp.logical_and(jnp.logical_and(relay, even), k < chunks))
+        def _():
+            pass_on(c)
 
         @pl.when(jnp.logical_and(even, k == chunks - 1))
         def _():
@@ -224,6 +279,12 @@
     for c in range(chunks):
         far_copy(c).wait_send()
         part_copy(c).wait_send()
+
+    @pl.when(relay)
+    def _():
+        for c in range(chunks):
+            relay_copy(c).wait_send()
+
     mate_copy.wait_send()
     mpart_copy.wait_send()
 
@@ -240,9 +301,10 @@
     return pl.pallas_call(
         functools.partial(kernel, n),
         out_shape=jax.ShapeDtypeStruct((cols, rows), F32),
-        in_specs=[pl.BlockSpec(memory_space=pl.ANY)] * 3,
+        in_specs=[pl.BlockSpec(memory_space=pltpu.HBM)] * 3,
         out_specs=vmem,
         scratch_shapes=[
+            pltpu.VMEM(packed, F32),
             pltpu.VMEM(packed, F32),
             pltpu.VMEM(packed, F32),
             pltpu.VMEM(packed, F32),
@@ -263,11 +325,11 @@
             pltpu.VMEM(turned, F32),
             pltpu.VMEM(turned, F32),
             sem((chunks, 1 + CHUNK // 128)), sem,
-            sem((chunks,)), sem((chunks,)), sem, sem,
+            sem((chunks,)), sem((chunks,)), sem((chunks,)), sem((chunks,)), sem, sem,
             sem((chunks,)), sem((chunks,)), sem, sem,
         ],
         compiler_params=pltpu.CompilerParams(
-            collective_id=0, has_side_effects=True, vmem_limit_bytes=48 * 1024 * 1024
+            collective_id=0, has_side_effects=True, vmem_limit_bytes=64 * 1024 * 1024 - 512 * 1024
         ),
     )(points, inv_scale[None, :], vectors.T).T
 

time: 50.1 us -> 51.9 us (1.036)
  the two profiles are of different devices: /device:TPU:6 before, /device:TPU:0 now
where the time goes in v4:
time: 51.9 us; the launch traced here: 51.7 us
  Pallas kernels  50 us (96%)
  local copies, waits for them, and re-layouts  1.77 us (3%)
    pallas_call x1, Pallas kernels, per_device(): pl.pallas_call(functools.partial(kernel, n), out_shape=jax.ShapeDtypeStru...  50 us
    unnamed x1, local copies, waits for them, and re-layouts  1.77 us

profile of v4, /device:TPU:0, one launch (start us, length us, event | category | flops | bytes accessed | tf_op | source)
XLA Modules:
  0.0 51.7 jit_solution(7592047762596879006)
XLA Ops:
  0.0 50.0 %shard_map.37 = f32[64,1536]{1,0:T(8,128)} custom-call(f32[1536,128]{1,0:T(8,128)} %p_ref.1, f32[1,128]{1,0:T(1,128)} %bitcast.5, f32[64,1536]{1,0:T(8,128)} %bitcast.4), custom_call_target="tpu_custom_call" | custom-call | tf_op jit(solution)/shard_map/pallas_call | solution.py:301
  50.0 1.8 %copy.5 = f32[1536,64]{0,1:T(8,128)} copy(f32[1536,64]{0,1:T(8,128)} %bitcast.3) | data formatting | bytes 786432

commit v5 on v3

--- a/solution.py
+++ b/solution.py
@@ -124,8 +124,7 @@
     )
     @pl.when(odd == 1)
     def _():
-        for c in range(chunks):
-            far_copy(c).start()
+        far_copy(0).start()
 
     mate_copy.start()
 
@@ -136,28 +135,38 @@
     lax.fori_loop(0, chunks, place_own, 0)
     acc_t[...] = jnp.zeros_like(acc_t)
 
-    def tile(a, c, b, mirrored):
+    def fill(a, c, b, first):
         col = jnp.concatenate([sq_col[a, c]] * (STRIP // 128), axis=1)
-        cross[...] = dot_nt(left[a, c], right[b])
-        for j in range(chunks * strips):
-            at = slice(j * STRIP, (j + 1) * STRIP)
+        cross[:, first:] = dot_nt(left[a, c], right[b, first:])
+        for start in range(first, chunks * CHUNK, STRIP):
+            at = slice(start, start + STRIP)
             values = jnp.exp2(cross[:, at] + col + sq_row[b, 0:1, at])
             tile_high[:, at], tile_low[:, at] = split(values)
-        total = dot(tile_high[...], vec[b]) + dot(tile_low[...], vec[b])
-        if mirrored:
-            acc_t[b] += dot(vec_t[a, c], tile_high[...]) + dot(vec_t[a, c], tile_low[...])
+        total = dot(tile_high[:, first:], vec[b, first:]) + dot(tile_low[:, first:], vec[b, first:])
         return fold(total.T)
 
-    def self_step(c, carry):
-        out_t[c] = tile(OWN, c, OWN, False)
-
-        @pl.when(even)
-        def _():
-            far_copy(c).start()
-
-        return carry
-
-    lax.fori_loop(0, chunks, self_step, 0)
+    def mirror(a, c, b, first):
+        acc_t[b, :, first:] += dot(vec_t[a, c], tile_high[:, first:]) + dot(
+            vec_t[a, c], tile_low[:, first:]
+        )
+
+    def tile(a, c, b):
+        part = fill(a, c, b, 0)
+        mirror(a, c, b, 0)
+        return part
+
+    for c in range(chunks):
+        out_t[c] = fill(OWN, c, OWN, c * CHUNK)
+        if c + 1 < chunks:
+            mirror(OWN, c, OWN, (c + 1) * CHUNK)
+
+        @pl.when(jnp.logical_and(odd == 1, c + 1 < chunks))
+        def _():
+            far_copy(min(c + 1, chunks - 1)).start()
+
+        @pl.when(jnp.logical_and(even, c >= 1))
+        def _():
+            far_copy(max(c - 1, 0)).start()
 
     mate_copy.wait_recv()
 
@@ -180,7 +189,7 @@
             far_copy(c).wait_recv()
             place(FAR, c, far_in)
 
-        part = tile(a, c, b, True)
+        part = tile(a, c, b)
 
         @pl.when(jnp.logical_not(uses_far))
         def _():
@@ -197,6 +206,10 @@
         @pl.when(jnp.where(even, k >= chunks, second == 1))
         def _():
             part_copy(c).start()
+
+        @pl.when(jnp.logical_and(even, k == 0))
+        def _():
+            far_copy(chunks - 1).start()
 
         @pl.when(jnp.logical_and(even, k == chunks - 1))
         def _():
@@ -240,7 +253,7 @@
     return pl.pallas_call(
         functools.partial(kernel, n),
         out_shape=jax.ShapeDtypeStruct((cols, rows), F32),
-        in_specs=[pl.BlockSpec(memory_space=pl.ANY)] * 3,
+        in_specs=[pl.BlockSpec(memory_space=pltpu.HBM)] * 3,
         out_specs=vmem,
         scratch_shapes=[
             pltpu.VMEM(packed, F32),
@@ -267,7 +280,7 @@
             sem((chunks,)), sem((chunks,)), sem, sem,
         ],
         compiler_params=pltpu.CompilerParams(
-            collective_id=0, has_side_effects=True, vmem_limit_bytes=48 * 1024 * 1024
+            collective_id=0, has_side_effects=True, vmem_limit_bytes=64 * 1024 * 1024 - 8192 * 1024
         ),
     )(points, inv_scale[None, :], vectors.T).T
 

time: 50.1 us -> 49.5 us (0.988)
  local copies, waits for them, and re-layouts: 3.53 us -> 1.77 us
  Pallas kernels: 46.3 us -> 47.5 us
    unnamed x7 -> x1, local copies, waits for them, and re-layouts: 3.53 us -> 1.77 us
    pallas_call x1, Pallas kernels: 46.3 us -> 47.5 us  [per_device(): pl.pallas_call(functools.partial(kernel, n), out_shape=jax.ShapeDtypeStru...]
where the time goes in v5:
time: 49.5 us; the launch traced here: 49.3 us
  Pallas kernels  47.5 us (96%)
  local copies, waits for them, and re-layouts  1.77 us (4%)
    pallas_call x1, Pallas kernels, per_device(): pl.pallas_call(functools.partial(kernel, n), out_shape=jax.ShapeDtypeStru...  47.5 us
    unnamed x1, local copies, waits for them, and re-layouts  1.77 us

profile of v5, /device:TPU:6, one launch (start us, length us, event | category | flops | bytes accessed | tf_op | source)
XLA Modules:
  0.0 49.3 jit_solution(8166520018533262230)
XLA Ops:
  0.0 47.5 %shard_map.37 = f32[64,1536]{1,0:T(8,128)} custom-call(f32[1536,128]{1,0:T(8,128)} %p_ref.1, f32[1,128]{1,0:T(1,128)} %bitcast.5, f32[64,1536]{1,0:T(8,128)} %bitcast.4), custom_call_target="tpu_custom_call" | custom-call | tf_op jit(solution)/shard_map/pallas_call | solution.py:253
  47.5 1.8 %copy.5 = f32[1536,64]{0,1:T(8,128)} copy(f32[1536,64]{0,1:T(8,128)} %bitcast.3) | data formatting | bytes 786432

commit v6 on v5

--- a/solution.py
+++ b/solution.py
@@ -164,9 +164,9 @@
         def _():
             far_copy(min(c + 1, chunks - 1)).start()
 
-        @pl.when(jnp.logical_and(even, c >= 1))
-        def _():
-            far_copy(max(c - 1, 0)).start()
+        @pl.when(even)
+        def _():
+            far_copy(c).start()
 
     mate_copy.wait_recv()
 
@@ -206,10 +206,6 @@
         @pl.when(jnp.where(even, k >= chunks, second == 1))
         def _():
             part_copy(c).start()
-
-        @pl.when(jnp.logical_and(even, k == 0))
-        def _():
-            far_copy(chunks - 1).start()
 
         @pl.when(jnp.logical_and(even, k == chunks - 1))
         def _():

time: 49.5 us -> 49.5 us (level)
  no operation moved by 1% of the time
where the time goes in v6:
time: 49.5 us; the launch traced here: 49.3 us
  Pallas kernels  47.5 us (96%)
  local copies, waits for them, and re-layouts  1.77 us (4%)
    pallas_call x1, Pallas kernels, per_device(): pl.pallas_call(functools.partial(kernel, n), out_shape=jax.ShapeDtypeStru...  47.5 us
    unnamed x1, local copies, waits for them, and re-layouts  1.77 us

profile of v6, /device:TPU:6, one launch (start us, length us, event | category | flops | bytes accessed | tf_op | source)
XLA Modules:
  0.0 49.3 jit_solution(10095473449776910375)
XLA Ops:
  0.0 47.5 %shard_map.37 = f32[64,1536]{1,0:T(8,128)} custom-call(f32[1536,128]{1,0:T(8,128)} %p_ref.1, f32[1,128]{1,0:T(1,128)} %bitcast.5, f32[64,1536]{1,0:T(8,128)} %bitcast.4), custom_call_target="tpu_custom_call" | custom-call | tf_op jit(solution)/shard_map/pallas_call | solution.py:249
  47.5 1.8 %copy.5 = f32[1536,64]{0,1:T(8,128)} copy(f32[1536,64]{0,1:T(8,128)} %bitcast.3) | data formatting | bytes 786432

commit v7 on v5

--- a/solution.py
+++ b/solution.py
@@ -124,7 +124,8 @@
     )
     @pl.when(odd == 1)
     def _():
-        far_copy(0).start()
+        for c in range(chunks):
+            far_copy(c).start()
 
     mate_copy.start()
 
@@ -159,10 +160,6 @@
         out_t[c] = fill(OWN, c, OWN, c * CHUNK)
         if c + 1 < chunks:
             mirror(OWN, c, OWN, (c + 1) * CHUNK)
-
-        @pl.when(jnp.logical_and(odd == 1, c + 1 < chunks))
-        def _():
-            far_copy(min(c + 1, chunks - 1)).start()
 
         @pl.when(jnp.logical_and(even, c >= 1))
         def _():

time: 49.5 us -> 49.5 us (level)
  no operation moved by 1% of the time
where the time goes in v7:
time: 49.5 us; the launch traced here: 49.3 us
  Pallas kernels  47.5 us (96%)
  local copies, waits for them, and re-layouts  1.77 us (4%)
    pallas_call x1, Pallas kernels, per_device(): pl.pallas_call(functools.partial(kernel, n), out_shape=jax.ShapeDtypeStru...  47.5 us
    unnamed x1, local copies, waits for them, and re-layouts  1.77 us

profile of v7, /device:TPU:6, one launch (start us, length us, event | category | flops | bytes accessed | tf_op | source)
XLA Modules:
  0.0 49.3 jit_solution(1062544172934213180)
XLA Ops:
  0.0 47.5 %shard_map.37 = f32[64,1536]{1,0:T(8,128)} custom-call(f32[1536,128]{1,0:T(8,128)} %p_ref.1, f32[1,128]{1,0:T(1,128)} %bitcast.5, f32[64,1536]{1,0:T(8,128)} %bitcast.4), custom_call_target="tpu_custom_call" | custom-call | tf_op jit(solution)/shard_map/pallas_call | solution.py:250
  47.5 1.8 %copy.5 = f32[1536,64]{0,1:T(8,128)} copy(f32[1536,64]{0,1:T(8,128)} %bitcast.3) | data formatting | bytes 786432
